TPU v7x, 32 devices: a whole 2x2x4 slice. The times are simulated.
32 devices in a mesh: dp: 2 (over core), seq: 16 (over z, y, x).
Axes of the slice: x: 2, y: 2, z: 4, core: 2. Of those that a mesh axis runs over, the one named last changes fastest.
Arguments:
- queries: bfloat16 [16384, 768], P(('dp', 'seq')), parts along dimension 0, may hold values from -11 to 11
- key_states: bfloat16 [16384, 768], P(('dp', 'seq')), parts along dimension 0, may hold values from -11 to 11
- value_states: bfloat16 [16384, 768], P(('dp', 'seq')), parts along dimension 0, may hold values from -6 to 6
- out_weight: bfloat16 [768, 1536], P('seq'), may hold values from -0.21875 to 0.21875
- block_picks: int32 [32, 6, 2], P(('dp', 'seq')), parts along dimension 0, may hold values from 0 to 3, as said below
- slot_counts: int32 [32, 6], P(('dp', 'seq')), parts along dimension 0, may hold values from 1 to 2, as said below
Outputs:
- projected: bfloat16 [16384, 1536], P(('dp', 'seq')), parts along dimension 0
There are 2 independent parts, one for each index of `dp`. A program takes and returns all parts, laid end to end along the dimension named above; an argument that names none is the same for every part. Nothing has to cross between parts.
Inputs may be any that keep to these rules, and one draw needn't show every extreme that they name: Each block_picks[s, j] holds 2 different spatial blocks of shard s. `slot_counts`: in every draw some shard has 2 in every direction.
All inputs are finite; a program needn't handle non-finite values.
Results may differ from a plain program's by a relative error of at most 0.0057.
Values may be sent and summed in bfloat16 or wider, within the bound.
A program may use at most 64 MiB of HBM per device.

v0:
```python
import jax
import jax.numpy as jnp
from jax import lax
from jax.sharding import PartitionSpec as P

HD = 128
BLOCK = 128
LEVELS = 3


def from_behind(block, axis, distance):
    devices = range(lax.axis_size(axis))
    route = [(i - distance, i) for i in devices if i - distance in devices]
    return lax.ppermute(block, axis, route)


def attend_rows(query_rows, key_rows, value_rows, key_live):
    head_total = query_rows.shape[1] // HD
    outputs = []
    for head_index in range(head_total):
        head_cols = slice(head_index * HD, (head_index + 1) * HD)
        scores = jnp.dot(
            query_rows[:, head_cols], key_rows[:, head_cols].T, preferred_element_type=jnp.float32
        ) * HD ** (-0.5)
        scores = jnp.where(key_live[None, :], scores, -jnp.inf)
        row_max = jnp.max(scores, axis=1, keepdims=True)
        weights = jnp.exp(scores - row_max)
        denominator = jnp.sum(weights, axis=1, keepdims=True)
        weighted = jnp.dot(
            weights.astype(jnp.bfloat16),
            value_rows[:, head_cols],
            preferred_element_type=jnp.float32,
        )
        outputs.append(weighted / denominator)
    return jnp.concatenate(outputs, axis=1).astype(jnp.bfloat16)


def shards(queries, key_states, value_states, out_weight, block_picks, slot_counts):
    tok_rows, feature_width = queries.shape
    block_len = BLOCK
    block_total = tok_rows // block_len
    level_count = LEVELS
    slot_count = block_picks.shape[2]
    stacked = jnp.stack([key_states, value_states]).reshape(
        2, block_total, block_len, feature_width
    )
    slot_ids = jnp.arange(slot_count, dtype=jnp.int32)
    packs = []
    marks = []
    for direction in range(2 * level_count):
        packs.append(jnp.take(stacked, block_picks[0, direction], axis=1))
        marks.append((slot_ids < slot_counts[0, direction]).astype(jnp.bfloat16))
    arrived_packs = [None] * (2 * level_count)
    arrived_marks = [None] * (2 * level_count)
    for direction in range(2 * level_count):
        hop_size = 2 ** (direction % level_count)
        direction_sign = 1 if direction < level_count else -1
        moved_pack, moved_mark = from_behind(
            (packs[direction], marks[direction]), "seq", direction_sign * hop_size
        )
        arrived_packs[direction] = moved_pack
        arrived_marks[direction] = moved_mark
    remote_keys = [
        pack_item[0].reshape(slot_count * block_len, feature_width) for pack_item in arrived_packs
    ]
    remote_values = [
        pack_item[1].reshape(slot_count * block_len, feature_width) for pack_item in arrived_packs
    ]
    remote_live = [jnp.repeat(mark_item > 0, block_len) for mark_item in arrived_marks]
    key_rows = jnp.concatenate([key_states] + remote_keys, axis=0)
    value_rows = jnp.concatenate([value_states] + remote_values, axis=0)
    key_live = jnp.concatenate([jnp.ones((tok_rows,), bool)] + remote_live, axis=0)
    attended = attend_rows(queries, key_rows, value_rows, key_live)
    result = jnp.dot(
        attended,
        lax.all_gather(out_weight, "seq", axis=0, tiled=True),
        preferred_element_type=jnp.float32,
    )
    return result.astype(jnp.bfloat16)


def solution(mesh):
    placed = (
        P(("dp", "seq"), None),
        P(("dp", "seq"), None),
        P(("dp", "seq"), None),
        P("seq", None),
        P(("dp", "seq"), None, None),
        P(("dp", "seq"), None),
    )
    return jax.shard_map(
        shards, mesh=mesh, in_specs=placed, out_specs=P(("dp", "seq"), None), check_vma=False
    )
```

profile of v0, /device:TPU:16, one launch (start us, length us, event | category | flops | bytes accessed | tf_op | source)
XLA Modules:
  0.0 195.9 jit_solution(12402553253930419312)
XLA Ops:
  10.9 3.4 %collective-permute-start.6 = (bf16[2,2,128,768]{3,2,0,1:T(8,128)(2,1)}, bf16[2,2,128,768]{3,2,0,1:T(8,128)(2,1)}, u32[]{:S(2)}, u32[]{:S(2)}) collective-permute-start(bf16[2,2,128,768]{3,2,0,1:T(8,128)(2,1)} %select_bitcast_fusion.5), channel_id=1, source_target_pairs={{0,1},{1,2},{2,3},{3,4},{4,5},{5,6},{6,7},{7,8},{8,9},{9,10},{10,1... | collective-permute-start | bytes 2359304 | tf_op jit(solution)/shard_map/ppermute | solution.py:14
  16.0 3.4 %collective-permute-start.7 = (bf16[2,2,128,768]{3,2,0,1:T(8,128)(2,1)}, bf16[2,2,128,768]{3,2,0,1:T(8,128)(2,1)}, u32[]{:S(2)}, u32[]{:S(2)}) collective-permute-start(bf16[2,2,128,768]{3,2,0,1:T(8,128)(2,1)} %select_bitcast_fusion.4), channel_id=1, source_target_pairs={{0,2},{1,3},{2,4},{3,5},{4,6},{5,7},{6,8},{7,9},{8,10},{9,11},{10,... | collective-permute-start | bytes 2359304 | tf_op jit(solution)/shard_map/ppermute | solution.py:14
  21.1 3.5 %collective-permute-start.8 = (bf16[2,2,128,768]{3,2,0,1:T(8,128)(2,1)}, bf16[2,2,128,768]{3,2,0,1:T(8,128)(2,1)}, u32[]{:S(2)}, u32[]{:S(2)}) collective-permute-start(bf16[2,2,128,768]{3,2,0,1:T(8,128)(2,1)} %select_bitcast_fusion.3), channel_id=1, source_target_pairs={{0,4},{1,5},{2,6},{3,7},{4,8},{5,9},{6,10},{7,11},{8,12},{9,13},{1... | collective-permute-start | bytes 2359304 | tf_op jit(solution)/shard_map/ppermute | solution.py:14
  26.3 4.2 %collective-permute-start.9 = (bf16[2,2,128,768]{3,2,0,1:T(8,128)(2,1)}, bf16[2,2,128,768]{3,2,0,1:T(8,128)(2,1)}, u32[]{:S(2)}, u32[]{:S(2)}) collective-permute-start(bf16[2,2,128,768]{3,2,0,1:T(8,128)(2,1)} %select_bitcast_fusion.2), channel_id=1, source_target_pairs={{1,0},{2,1},{3,2},{4,3},{5,4},{6,5},{7,6},{8,7},{9,8},{10,9},{11,1... | collective-permute-start | bytes 2359304 | tf_op jit(solution)/shard_map/ppermute | solution.py:14
  31.9 1.9 collective-permute-start
  34.8 2.1 %constant_dynamic-update-slice_fusion.13 = bf16[2048,768]{1,0:T(8,128)(2,1)} fusion(bf16[512,768]{1,0:T(8,128)(2,1)} %param.10), kind=kLoop, calls=%fused_computation.111 | loop fusion | bytes 1572864
  43.3 2.2 %select_bitcast_fusion.1 = bf16[2,2,128,768]{3,2,0,1:T(8,128)(2,1)} fusion(bf16[2,2,128,768]{3,2,1,0:T(8,128)(2,1)} %gather_fusion.4, pred[2]{0:T(512)(128)(4,1)S(1)} %compare_and_fusion.1), kind=kLoop, calls=%fused_computation.69 | loop fusion | flops 393216 | bytes 1572866 | tf_op jit(solution)/shard_map/jit(_take)/select_n | solution.py:51
  45.5 2.2 %select_bitcast_fusion = bf16[2,2,128,768]{3,2,0,1:T(8,128)(2,1)} fusion(bf16[2,2,128,768]{3,2,1,0:T(8,128)(2,1)} %gather_fusion.5, pred[2]{0:T(512)(128)(4,1)S(1)} %compare_and_fusion), kind=kLoop, calls=%fused_computation.68 | loop fusion | flops 393216 | bytes 1572866 | tf_op jit(solution)/shard_map/jit(_take)/select_n | solution.py:51
  47.9 39.1 %collective-permute-done = bf16[2]{0:T(256)(128)(2,1)S(1)} collective-permute-done((bf16[2]{0:T(256)(128)(2,1)S(1)}, bf16[2]{0:T(256)(128)(2,1)S(1)}, u32[]{:S(2)}, u32[]{:S(2)}) %collective-permute-start) | collective-permute-done | bytes 36 | tf_op jit(solution)/shard_map/ppermute | solution.py:14
  87.0 1.9 collective-permute-start.1
  89.0 4.3 %collective-permute-done.1 = bf16[2]{0:T(256)(128)(2,1)S(1)} collective-permute-done((bf16[2]{0:T(256)(128)(2,1)S(1)}, bf16[2]{0:T(256)(128)(2,1)S(1)}, u32[]{:S(2)}, u32[]{:S(2)}) %collective-permute-start.1) | collective-permute-done | bytes 36 | tf_op jit(solution)/shard_map/ppermute | solution.py:14
  93.3 3.8 %collective-permute-start.2 = (bf16[2]{0:T(256)(128)(2,1)S(1)}, bf16[2]{0:T(256)(128)(2,1)S(1)}, u32[]{:S(2)}, u32[]{:S(2)}) collective-permute-start(bf16[2]{0:T(256)(128)(2,1)S(1)} %compare_convert_fusion.3), channel_id=1, source_target_pairs={{0,4},{1,5},{2,6},{3,7},{4,8},{5,9},{6,10},{7,11},{8,12},{9,13},{1... | collective-permute-start | bytes 20 | tf_op jit(solution)/shard_map/ppermute | solution.py:14
  98.7 1.9 collective-permute-start.3
  100.7 3.4 %collective-permute-done.3 = bf16[2]{0:T(256)(128)(2,1)S(1)} collective-permute-done((bf16[2]{0:T(256)(128)(2,1)S(1)}, bf16[2]{0:T(256)(128)(2,1)S(1)}, u32[]{:S(2)}, u32[]{:S(2)}) %collective-permute-start.3) | collective-permute-done | bytes 36 | tf_op jit(solution)/shard_map/ppermute | solution.py:14
  104.1 1.9 collective-permute-start.4
  106.2 3.4 %collective-permute-done.4 = bf16[2]{0:T(256)(128)(2,1)S(1)} collective-permute-done((bf16[2]{0:T(256)(128)(2,1)S(1)}, bf16[2]{0:T(256)(128)(2,1)S(1)}, u32[]{:S(2)}, u32[]{:S(2)}) %collective-permute-start.4) | collective-permute-done | bytes 36 | tf_op jit(solution)/shard_map/ppermute | solution.py:14
  109.6 2.2 %collective-permute-start.5 = (bf16[2]{0:T(256)(128)(2,1)S(1)}, bf16[2]{0:T(256)(128)(2,1)S(1)}, u32[]{:S(2)}, u32[]{:S(2)}) collective-permute-start(bf16[2]{0:T(256)(128)(2,1)S(1)} %compare_convert_fusion), channel_id=1, source_target_pairs={{4,0},{5,1},{6,2},{7,3},{8,4},{9,5},{10,6},{11,7},{12,8},{13,9},{1... | collective-permute-start | bytes 20 | tf_op jit(solution)/shard_map/ppermute | solution.py:14
  111.8 3.2 %collective-permute-done.5 = bf16[2]{0:T(256)(128)(2,1)S(1)} collective-permute-done((bf16[2]{0:T(256)(128)(2,1)S(1)}, bf16[2]{0:T(256)(128)(2,1)S(1)}, u32[]{:S(2)}, u32[]{:S(2)}) %collective-permute-start.5) | collective-permute-done | bytes 36 | tf_op jit(solution)/shard_map/ppermute | solution.py:14
  115.0 2.9 %collective-permute-start.10 = (bf16[2,2,128,768]{3,2,0,1:T(8,128)(2,1)}, bf16[2,2,128,768]{3,2,0,1:T(8,128)(2,1)}, u32[]{:S(2)}, u32[]{:S(2)}) collective-permute-start(bf16[2,2,128,768]{3,2,0,1:T(8,128)(2,1)} %select_bitcast_fusion.1), channel_id=1, source_target_pairs={{2,0},{3,1},{4,2},{5,3},{6,4},{7,5},{8,6},{9,7},{10,8},{11,9},{12,... | collective-permute-start | bytes 2359304 | tf_op jit(solution)/shard_map/ppermute | solution.py:14
  119.1 2.5 %collective-permute-start.11 = (bf16[2,2,128,768]{3,2,0,1:T(8,128)(2,1)}, bf16[2,2,128,768]{3,2,0,1:T(8,128)(2,1)S(1)}, u32[]{:S(2)}, u32[]{:S(2)}) collective-permute-start(bf16[2,2,128,768]{3,2,0,1:T(8,128)(2,1)} %select_bitcast_fusion), channel_id=1, source_target_pairs={{4,0},{5,1},{6,2},{7,3},{8,4},{9,5},{10,6},{11,7},{12,8},{13,9},{1... | collective-permute-start | bytes 2359304 | tf_op jit(solution)/shard_map/ppermute | solution.py:14
  122.9 1.9 fusion.130
  124.8 1.9 fusion.129
  126.8 2.0 %fusion.128 = (bf16[1,2,128,768]{3,2,0,1:T(8,128)(2,1)}, bf16[1,2,128,768]{3,2,0,1:T(8,128)(2,1)S(1)}) fusion(bf16[2,2,128,768]{3,2,0,1:T(8,128)(2,1)} %collective-permute-done.9), kind=kLoop, calls=%fused_computation.168 | loop fusion | bytes 1572864 | tf_op jit(solution)/shard_map/slice | solution.py:67
  128.8 7.4 %collective-permute-done.10 = bf16[2,2,128,768]{3,2,0,1:T(8,128)(2,1)} collective-permute-done((bf16[2,2,128,768]{3,2,0,1:T(8,128)(2,1)}, bf16[2,2,128,768]{3,2,0,1:T(8,128)(2,1)}, u32[]{:S(2)}, u32[]{:S(2)}) %collective-permute-start.10) | collective-permute-done | bytes 786464 | tf_op jit(solution)/shard_map/ppermute | solution.py:14
  136.2 1.9 fusion.127
  138.1 12.2 %collective-permute-done.11 = bf16[2,2,128,768]{3,2,0,1:T(8,128)(2,1)S(1)} collective-permute-done((bf16[2,2,128,768]{3,2,0,1:T(8,128)(2,1)}, bf16[2,2,128,768]{3,2,0,1:T(8,128)(2,1)S(1)}, u32[]{:S(2)}, u32[]{:S(2)}) %collective-permute-start.11) | collective-permute-done | bytes 786464 | tf_op jit(solution)/shard_map/ppermute | solution.py:14
  155.6 5.6 %fusion.16 = (f32[512]{0:T(512)}, f32[512]{0:T(512)}, f32[512]{0:T(512)}, f32[512]{0:T(512)S(1)}, f32[512]{0:T(512)S(1)}, /*index=5*/f32[512]{0:T(512)}, f32[2048,512]{1,0:T(8,128)S(1)}) fusion(f32[2048,512]{1,0:T(8,128)S(1)} %get-tuple-element.42, f32[512]{0:T(512)S(1)} %get-tuple-element.12, pred[2048]{0:T(1024)(128)(4,1)S(1)} %dynamic-update-slice.26, ...), kind=kOutput, calls=%fused_computation.34 | convolution fusion | flops 289403904 | bytes 25839616 | tf_op jit(solution)/shard_map/dot_general | solution.py:22
  162.0 1.8 constant_dynamic-update-slice_fusion.11
  165.5 1.8 constant_dynamic-update-slice_fusion.9
  169.9 2.5 %fusion.42 = bf16[512,768]{1,0:T(8,128)(2,1)S(1)} fusion(f32[2048,512]{1,0:T(8,128)S(1)} %fusion.106, f32[512]{0:T(512)S(1)} %copy-done.9, pred[2048]{0:T(1024)(128)(4,1)S(1)} %dynamic-update-slice.26, bf16[2048,768]{1,0:T(8,128)(2,1)} %constant_dynamic-update-slice_fusion.7, f32[512]{0:T(512)S(1)} %copy-done.11), kind=kOutput, calls=%fused_computation.52 | convolution fusion | flops 272760832 | bytes 4855808 | tf_op jit(solution)/shard_map/dot_general | solution.py:29
  172.4 4.9 %fusion.14 = (f32[512]{0:T(512)S(1)}, f32[512]{0:T(512)S(1)}, f32[512]{0:T(512)S(1)}, f32[512]{0:T(512)S(1)}) fusion(f32[2048,512]{1,0:T(8,128)S(1)} %fusion.94, f32[512]{0:T(512)S(1)} %get-tuple-element.10, pred[2048]{0:T(1024)(128)(4,1)S(1)} %dynamic-update-slice.26, f32[512]{0:T(512)S(1)} %copy-done.7, f32[2048,512]{1,0:T(8,128)S(1)} %get-tuple-element.43, ...), kind=kLoop, calls=%fused_computation.32 | loop fusion | flops 16775168 | bytes 16795648 | tf_op jit(solution)/shard_map/reduce_sum | solution.py:28
  184.9 4.2 %convolution_convert_fusion = bf16[512,1536]{1,0:T(8,128)(2,1)} fusion(bf16[512,768]{1,0:T(8,128)(2,1)S(1)} %fusion.87, bf16[768,1536]{1,0:T(8,128)(2,1)} %all-gather.2.cloned.1.call-done), kind=kOutput, calls=%fused_computation.36 | convolution fusion | flops 1208745984 | bytes 4718592 | tf_op jit(solution)/shard_map/dot_general | solution.py:74
  (110 shorter events, 40.7 us)
Async XLA Ops:
  6.5 178.4 %all-gather.2.cloned.1.call-start = ((), (), s32[]{:S(2)}) async-start(), calls=%async_computation | async-start | bytes 2506752 | tf_op jit(solution)/shard_map/all_gather | solution.py:76
  10.9 108.3 %collective-permute-start.6 = (bf16[2,2,128,768]{3,2,0,1:T(8,128)(2,1)}, bf16[2,2,128,768]{3,2,0,1:T(8,128)(2,1)}, u32[]{:S(2)}, u32[]{:S(2)}) collective-permute-start(bf16[2,2,128,768]{3,2,0,1:T(8,128)(2,1)} %select_bitcast_fusion.5), channel_id=1, source_target_pairs={{0,1},{1,2},{2,3},{3,4},{4,5},{5,6},{6,7},{7,8},{8,9},{9,10},{10,1... | collective-permute-start | bytes 2359304 | tf_op jit(solution)/shard_map/ppermute | solution.py:14
  14.9 15.6 %copy-start.5 = (s32[1,6]{1,0:T(1,128)S(1)}, s32[1,6]{1,0:T(1,128)}, u32[]{:S(2)}) copy-start(s32[1,6]{1,0:T(1,128)} %param.13) | copy-start | bytes 76
  14.9 18.9 %copy-start.1 = (bf16[512,768]{1,0:T(8,128)(2,1)S(1)}, bf16[512,768]{1,0:T(8,128)(2,1)}, u32[]{:S(2)}) copy-start(bf16[512,768]{1,0:T(8,128)(2,1)} %param.9) | copy-start | bytes 2359300
  16.0 106.9 %collective-permute-start.7 = (bf16[2,2,128,768]{3,2,0,1:T(8,128)(2,1)}, bf16[2,2,128,768]{3,2,0,1:T(8,128)(2,1)}, u32[]{:S(2)}, u32[]{:S(2)}) collective-permute-start(bf16[2,2,128,768]{3,2,0,1:T(8,128)(2,1)} %select_bitcast_fusion.4), channel_id=1, source_target_pairs={{0,2},{1,3},{2,4},{3,5},{4,6},{5,7},{6,8},{7,9},{8,10},{9,11},{10,... | collective-permute-start | bytes 2359304 | tf_op jit(solution)/shard_map/ppermute | solution.py:14
  21.1 103.7 %collective-permute-start.8 = (bf16[2,2,128,768]{3,2,0,1:T(8,128)(2,1)}, bf16[2,2,128,768]{3,2,0,1:T(8,128)(2,1)}, u32[]{:S(2)}, u32[]{:S(2)}) collective-permute-start(bf16[2,2,128,768]{3,2,0,1:T(8,128)(2,1)} %select_bitcast_fusion.3), channel_id=1, source_target_pairs={{0,4},{1,5},{2,6},{3,7},{4,8},{5,9},{6,10},{7,11},{8,12},{9,13},{1... | collective-permute-start | bytes 2359304 | tf_op jit(solution)/shard_map/ppermute | solution.py:14
  26.3 100.5 %collective-permute-start.9 = (bf16[2,2,128,768]{3,2,0,1:T(8,128)(2,1)}, bf16[2,2,128,768]{3,2,0,1:T(8,128)(2,1)}, u32[]{:S(2)}, u32[]{:S(2)}) collective-permute-start(bf16[2,2,128,768]{3,2,0,1:T(8,128)(2,1)} %select_bitcast_fusion.2), channel_id=1, source_target_pairs={{1,0},{2,1},{3,2},{4,3},{5,4},{6,5},{7,6},{8,7},{9,8},{10,9},{11,1... | collective-permute-start | bytes 2359304 | tf_op jit(solution)/shard_map/ppermute | solution.py:14
  31.9 55.1 %collective-permute-start = (bf16[2]{0:T(256)(128)(2,1)S(1)}, bf16[2]{0:T(256)(128)(2,1)S(1)}, u32[]{:S(2)}, u32[]{:S(2)}) collective-permute-start(bf16[2]{0:T(256)(128)(2,1)S(1)} %compare_convert_fusion.5), channel_id=1, source_target_pairs={{0,1},{1,2},{2,3},{3,4},{4,5},{5,6},{6,7},{7,8},{8,9},{9,10},{10,1... | collective-permute-start | bytes 20 | tf_op jit(solution)/shard_map/ppermute | solution.py:14
  39.9 82.9 %copy-start = (bf16[2048,768]{1,0:T(8,128)(2,1)S(1)}, bf16[2048,768]{1,0:T(8,128)(2,1)}, u32[]{:S(2)}) copy-start(bf16[2048,768]{1,0:T(8,128)(2,1)} %constant_dynamic-update-slice_fusion.6) | copy-start | bytes 9437188
  87.0 6.3 %collective-permute-start.1 = (bf16[2]{0:T(256)(128)(2,1)S(1)}, bf16[2]{0:T(256)(128)(2,1)S(1)}, u32[]{:S(2)}, u32[]{:S(2)}) collective-permute-start(bf16[2]{0:T(256)(128)(2,1)S(1)} %compare_convert_fusion.4), channel_id=1, source_target_pairs={{0,2},{1,3},{2,4},{3,5},{4,6},{5,7},{6,8},{7,9},{8,10},{9,11},{10,... | collective-permute-start | bytes 20 | tf_op jit(solution)/shard_map/ppermute | solution.py:14
  93.3 5.4 %collective-permute-start.2 = (bf16[2]{0:T(256)(128)(2,1)S(1)}, bf16[2]{0:T(256)(128)(2,1)S(1)}, u32[]{:S(2)}, u32[]{:S(2)}) collective-permute-start(bf16[2]{0:T(256)(128)(2,1)S(1)} %compare_convert_fusion.3), channel_id=1, source_target_pairs={{0,4},{1,5},{2,6},{3,7},{4,8},{5,9},{6,10},{7,11},{8,12},{9,13},{1... | collective-permute-start | bytes 20 | tf_op jit(solution)/shard_map/ppermute | solution.py:14
  98.7 5.4 %collective-permute-start.3 = (bf16[2]{0:T(256)(128)(2,1)S(1)}, bf16[2]{0:T(256)(128)(2,1)S(1)}, u32[]{:S(2)}, u32[]{:S(2)}) collective-permute-start(bf16[2]{0:T(256)(128)(2,1)S(1)} %compare_convert_fusion.2), channel_id=1, source_target_pairs={{1,0},{2,1},{3,2},{4,3},{5,4},{6,5},{7,6},{8,7},{9,8},{10,9},{11,1... | collective-permute-start | bytes 20 | tf_op jit(solution)/shard_map/ppermute | solution.py:14
  104.1 5.4 %collective-permute-start.4 = (bf16[2]{0:T(256)(128)(2,1)S(1)}, bf16[2]{0:T(256)(128)(2,1)S(1)}, u32[]{:S(2)}, u32[]{:S(2)}) collective-permute-start(bf16[2]{0:T(256)(128)(2,1)S(1)} %compare_convert_fusion.1), channel_id=1, source_target_pairs={{2,0},{3,1},{4,2},{5,3},{6,4},{7,5},{8,6},{9,7},{10,8},{11,9},{12,... | collective-permute-start | bytes 20 | tf_op jit(solution)/shard_map/ppermute | solution.py:14
  109.6 5.4 %collective-permute-start.5 = (bf16[2]{0:T(256)(128)(2,1)S(1)}, bf16[2]{0:T(256)(128)(2,1)S(1)}, u32[]{:S(2)}, u32[]{:S(2)}) collective-permute-start(bf16[2]{0:T(256)(128)(2,1)S(1)} %compare_convert_fusion), channel_id=1, source_target_pairs={{4,0},{5,1},{6,2},{7,3},{8,4},{9,5},{10,6},{11,7},{12,8},{13,9},{1... | collective-permute-start | bytes 20 | tf_op jit(solution)/shard_map/ppermute | solution.py:14
  115.0 21.2 %collective-permute-start.10 = (bf16[2,2,128,768]{3,2,0,1:T(8,128)(2,1)}, bf16[2,2,128,768]{3,2,0,1:T(8,128)(2,1)}, u32[]{:S(2)}, u32[]{:S(2)}) collective-permute-start(bf16[2,2,128,768]{3,2,0,1:T(8,128)(2,1)} %select_bitcast_fusion.1), channel_id=1, source_target_pairs={{2,0},{3,1},{4,2},{5,3},{6,4},{7,5},{8,6},{9,7},{10,8},{11,9},{12,... | collective-permute-start | bytes 2359304 | tf_op jit(solution)/shard_map/ppermute | solution.py:14
  119.1 31.1 %collective-permute-start.11 = (bf16[2,2,128,768]{3,2,0,1:T(8,128)(2,1)}, bf16[2,2,128,768]{3,2,0,1:T(8,128)(2,1)S(1)}, u32[]{:S(2)}, u32[]{:S(2)}) collective-permute-start(bf16[2,2,128,768]{3,2,0,1:T(8,128)(2,1)} %select_bitcast_fusion), channel_id=1, source_target_pairs={{4,0},{5,1},{6,2},{7,3},{8,4},{9,5},{10,6},{11,7},{12,8},{13,9},{1... | collective-permute-start | bytes 2359304 | tf_op jit(solution)/shard_map/ppermute | solution.py:14
  126.7 24.4 %copy-start.3 = (bf16[512,768]{1,0:T(8,128)(2,1)S(1)}, bf16[512,768]{1,0:T(8,128)(2,1)}, u32[]{:S(2)}) copy-start(bf16[512,768]{1,0:T(8,128)(2,1)} %param.8) | copy-start | bytes 2359300
  155.0 0.6 copy-start.8
  161.2 7.9 %copy-start.2 = (bf16[1,2,128,768]{3,2,0,1:T(8,128)(2,1)S(1)}, bf16[1,2,128,768]{3,2,0,1:T(8,128)(2,1)}, u32[]{:S(2)}) copy-start(bf16[1,2,128,768]{3,2,0,1:T(8,128)(2,1)} %get-tuple-element.24) | copy-start | bytes 1179652
  161.2 8.7 %copy-start.9 = (f32[512]{0:T(512)S(1)}, f32[512]{0:T(512)}, u32[]{:S(2)}) copy-start(f32[512]{0:T(512)} %copy-done.8) | copy-start | bytes 6148
  161.2 8.7 %copy-start.11 = (f32[512]{0:T(512)S(1)}, f32[512]{0:T(512)}, u32[]{:S(2)}) copy-start(f32[512]{0:T(512)} %get-tuple-element.11) | copy-start | bytes 6148
  169.1 3.3 %copy-start.6 = (f32[512]{0:T(512)S(1)}, f32[512]{0:T(512)}, u32[]{:S(2)}) copy-start(f32[512]{0:T(512)} %get-tuple-element.8) | copy-start | bytes 6148
  169.1 3.3 %copy-start.7 = (f32[512]{0:T(512)S(1)}, f32[512]{0:T(512)}, u32[]{:S(2)}) copy-start(f32[512]{0:T(512)} %get-tuple-element.7) | copy-start | bytes 6148
  172.4 4.9 %copy-start.4 = (bf16[2048,768]{1,0:T(8,128)(2,1)S(1)}, bf16[2048,768]{1,0:T(8,128)(2,1)}, u32[]{:S(2)}) copy-start(bf16[2048,768]{1,0:T(8,128)(2,1)} %constant_dynamic-update-slice_fusion.7) | copy-start | bytes 9437188
  181.8 1.5 copy-start.10
Sparse Core Ops, SparseCore 0:
  34.0 85.6 all-gather.1
where the time goes:
time: 199 us; the launch traced here: 196 us
  waiting for transfers between devices  74.5 us (37%)
  starting transfers between devices  33.5 us (17%)
  local copies, waits for them, and re-layouts  31.1 us (16%)
  matrix products  23.7 us (12%)
  other arithmetic  19.1 us (10%)
  between operations  13.9 us (7%)
    ppermute x12, waiting for transfers between devices, from_behind(): return lax.ppermute(block, axis, route)  74.4 us
    ppermute x12, starting transfers between devices, from_behind(): return lax.ppermute(block, axis, route)  33.5 us
    unnamed x42, local copies, waits for them, and re-layouts  12.8 us
    dot_general x6, matrix products, attend_rows(): jnp.dot(weights.astype(jnp.bfloat16), value_rows[:, head_cols], preferred...  10 us
    slice x6, local copies, waits for them, and re-layouts, shards(): pack_item[1].reshape(slot_count * block_len, feature_width)  9.69 us
    dot_general x6, matrix products, attend_rows(): jnp.dot(query_rows[:, head_cols], key_rows[:, head_cols].T, preferred_ele...  9.48 us
    select_n x12, other arithmetic, shards(): packs.append(jnp.take(stacked, block_picks[0, direction], axis=1))  8.57 us
    gather x6, local copies, waits for them, and re-layouts, shards(): packs.append(jnp.take(stacked, block_picks[0, direction], axis=1))  5.38 us
  transfers between devices with their start and end apart: 13, of which 8 were waited for; matrix products, arithmetic and copies ran while one was open for 33% of the time, Pallas kernels for 0%

commit v1 on v0

v1 whole, which is shorter than its diff:
```python
import functools

import jax
import jax.numpy as jnp
from jax import lax
from jax.experimental import pallas as pl
from jax.experimental.pallas import tpu as pltpu
from jax.sharding import PartitionSpec as P

HD = 128
BLOCK = 128
LEVELS = 3
DIRS = 2 * LEVELS
MASKED = -1e30
SEND_ORDER = (1, 4, 0, 3, 2, 5)
WORK_ORDER = (2, 5, 0, 3, 1, 4)


def hop(direction):
    size = 2 ** (direction % LEVELS)
    return size if direction < LEVELS else -size


def kernel(
    n, q_ref, k_ref, v_ref, w_ref, picks_ref, counts_ref, out_ref, wout_ref,
    pack, mark, got, got_mark, acc, top, total,
    pack_send, pack_recv, mark_send, mark_recv, w_send, w_recv, own_sem, pair_send, pair_recv,
):
    me = lax.axis_index("seq")
    dp = lax.axis_index("dp")
    sibling = dp + 1 - 2 * (dp % 2)
    rows, width = q_ref.shape
    heads = width // HD
    slots = picks_ref.shape[1]
    bits = n.bit_length() - 1
    half_cols = w_ref.shape[1] // 2
    half = pl.ds(pl.multiple_of((dp % 2) * half_cols, half_cols), half_cols)

    def partner(bit):
        return me + 2**bit * (1 - 2 * ((me // 2**bit) % 2))

    def inside(shard):
        return jnp.logical_and(shard >= 0, shard < n)

    barrier = pltpu.get_barrier_semaphore()
    expected = jnp.int32(bits + 1)
    for direction in range(DIRS):
        other = me + hop(direction)
        expected = expected + inside(other).astype(jnp.int32)

        @pl.when(inside(other))
        def _(other=other):
            pl.semaphore_signal(
                barrier, inc=1, device_id=(dp, other), device_id_type=pl.DeviceIdType.MESH
            )
    for bit in range(bits):
        pl.semaphore_signal(
            barrier, inc=1, device_id=(dp, partner(bit)), device_id_type=pl.DeviceIdType.MESH
        )
    pl.semaphore_signal(
        barrier, inc=1, device_id=(sibling, me), device_id_type=pl.DeviceIdType.MESH
    )

    own = pltpu.make_async_copy(w_ref.at[:, half], wout_ref.at[me, :, half], own_sem)
    own.start()

    def fill(direction):
        for slot in range(slots):
            block = picks_ref[direction, slot]
            at = pl.ds(slot * BLOCK, BLOCK)
            pack[direction, 0, at, :] = k_ref[block]
            pack[direction, 1, at, :] = v_ref[block]
            live = counts_ref[0, direction] > slot
            mark[direction, slot] = jnp.full((8, HD), jnp.where(live, 0.0, MASKED), jnp.float32)

    def pack_copies(direction):
        to = (dp, me + hop(direction))
        return (
            pltpu.make_async_remote_copy(
                pack.at[direction], got.at[direction],
                pack_send.at[direction], pack_recv.at[direction],
                device_id=to, device_id_type=pl.DeviceIdType.MESH,
            ),
            pltpu.make_async_remote_copy(
                mark.at[direction], got_mark.at[direction],
                mark_send.at[direction], mark_recv.at[direction],
                device_id=to, device_id_type=pl.DeviceIdType.MESH,
            ),
        )

    def weight_copies(step):
        bit = bits - 1 - step
        span = 2 ** (bit + 1)
        copies = []
        for i in range(2**step):
            place = wout_ref.at[me % span + i * span, :, half]
            index = 2**step - 1 + i
            copies.append(
                pltpu.make_async_remote_copy(
                    place, place, w_send.at[index], w_recv.at[index],
                    device_id=(dp, partner(bit)), device_id_type=pl.DeviceIdType.MESH,
                )
            )
        return copies

    pair = pltpu.make_async_remote_copy(
        wout_ref.at[:, :, half], wout_ref.at[:, :, half], pair_send, pair_recv,
        device_id=(sibling, me), device_id_type=pl.DeviceIdType.MESH,
    )

    def weight_step(step):
        if step > bits:
            return
        if step > 0:
            for copy in weight_copies(step - 1):
                copy.wait_recv()
        if step < bits:
            for copy in weight_copies(step):
                copy.start()
        else:
            pair.start()

    fill(SEND_ORDER[0])
    pl.semaphore_wait(barrier, expected)
    for place, direction in enumerate(SEND_ORDER):
        if place > 0:
            fill(direction)

        @pl.when(inside(me + hop(direction)))
        def _(direction=direction):
            for copy in pack_copies(direction):
                copy.start()

        if place == 0:
            own.wait()
            weight_step(0)

    scale = HD**-0.5
    tiles = 2
    tile = rows // tiles

    def local_head(h, carry):
        cols = pl.ds(pl.multiple_of(h * HD, HD), HD)
        keys = k_ref[:, :, cols].reshape(rows, HD)
        values = v_ref[:, :, cols].reshape(rows, HD)
        for t in range(tiles):
            at = pl.ds(t * tile, tile)
            scores = lax.dot_general(
                q_ref[at, cols], keys, (((1,), (1,)), ((), ())),
                preferred_element_type=jnp.float32,
            ) * scale
            high = jnp.max(scores, axis=1, keepdims=True)
            weights = jnp.exp(scores - high)
            top[h, at, :] = high
            total[h, at, :] = jnp.sum(weights, axis=1, keepdims=True)
            acc[h, at, :] = jnp.dot(
                weights.astype(jnp.bfloat16), values, preferred_element_type=jnp.float32
            )
        return carry

    lax.fori_loop(0, heads, local_head, 0)
    weight_step(1)

    def far_head(direction, h):
        cols = pl.ds(pl.multiple_of(h * HD, HD), HD)
        keys = got[direction, 0, :, cols]
        values = got[direction, 1, :, cols]
        bias = jnp.concatenate(
            [got_mark[direction, slot, 0:1, :] for slot in range(slots)], axis=1
        )
        for t in range(tiles):
            at = pl.ds(t * tile, tile)
            scores = lax.dot_general(
                q_ref[at, cols], keys, (((1,), (1,)), ((), ())),
                preferred_element_type=jnp.float32,
            ) * scale + bias
            before = top[h, at, :]
            high = jnp.maximum(before, jnp.max(scores, axis=1, keepdims=True))
            shrink = jnp.exp(before - high)
            weights = jnp.exp(scores - high)
            top[h, at, :] = high
            total[h, at, :] = total[h, at, :] * shrink + jnp.sum(weights, axis=1, keepdims=True)
            acc[h, at, :] = acc[h, at, :] * shrink + jnp.dot(
                weights.astype(jnp.bfloat16), values, preferred_element_type=jnp.float32
            )

    for place, direction in enumerate(WORK_ORDER):

        @pl.when(inside(me - hop(direction)))
        def _(direction=direction):
            for copy in pack_copies(direction):
                copy.wait_recv()

            def body(h, carry):
                far_head(direction, h)
                return carry

            lax.fori_loop(0, heads, body, 0)

        weight_step(place + 2)
    for step in range(DIRS + 2, bits + 1):
        weight_step(step)

    for h in range(heads):
        out_ref[:, h * HD : (h + 1) * HD] = (acc[h] / total[h]).astype(out_ref.dtype)

    for direction in range(DIRS):

        @pl.when(inside(me + hop(direction)))
        def _(direction=direction):
            for copy in pack_copies(direction):
                copy.wait_send()

    for step in range(bits):
        for copy in weight_copies(step):
            copy.wait_send()
    pair.wait()


def shards(queries, key_states, value_states, out_weight, block_picks, slot_counts):
    n = lax.axis_size("seq")
    rows, width = queries.shape
    slots = block_picks.shape[2]
    heads = width // HD
    blocks = rows // BLOCK
    vmem = pl.BlockSpec(memory_space=pltpu.VMEM)
    smem = pl.BlockSpec(memory_space=pltpu.SMEM)
    dma = pltpu.SemaphoreType.DMA
    attended, weight = pl.pallas_call(
        functools.partial(kernel, n),
        out_shape=(
            jax.ShapeDtypeStruct((rows, width), jnp.bfloat16),
            jax.ShapeDtypeStruct((n,) + out_weight.shape, jnp.bfloat16),
        ),
        in_specs=[vmem, vmem, vmem, vmem, smem, smem],
        out_specs=(vmem, pl.BlockSpec(memory_space=pl.ANY)),
        scratch_shapes=[
            pltpu.VMEM((DIRS, 2, slots * BLOCK, width), jnp.bfloat16),
            pltpu.VMEM((DIRS, slots, 8, HD), jnp.float32),
            pltpu.VMEM((DIRS, 2, slots * BLOCK, width), jnp.bfloat16),
            pltpu.VMEM((DIRS, slots, 8, HD), jnp.float32),
            pltpu.VMEM((heads, rows, HD), jnp.float32),
            pltpu.VMEM((heads, rows, 1), jnp.float32),
            pltpu.VMEM((heads, rows, 1), jnp.float32),
            dma((DIRS,)), dma((DIRS,)), dma((DIRS,)), dma((DIRS,)),
            dma((n,)), dma((n,)), dma, dma, dma,
        ],
        compiler_params=pltpu.CompilerParams(
            collective_id=0, has_side_effects=True, vmem_limit_bytes=48 * 2**20
        ),
    )(
        queries,
        key_states.reshape(blocks, BLOCK, width),
        value_states.reshape(blocks, BLOCK, width),
        out_weight,
        block_picks[0],
        slot_counts,
    )
    result = jnp.dot(
        attended, weight.reshape(-1, weight.shape[2]), preferred_element_type=jnp.float32
    )
    return result.astype(jnp.bfloat16)


def solution(mesh):
    placed = (
        P(("dp", "seq"), None),
        P(("dp", "seq"), None),
        P(("dp", "seq"), None),
        P("seq", None),
        P(("dp", "seq"), None, None),
        P(("dp", "seq"), None),
    )
    return jax.shard_map(
        shards, mesh=mesh, in_specs=placed, out_specs=P(("dp", "seq"), None), check_vma=False
    )
```

time: 199 us -> 121 us (0.61)
  the two profiles are of different devices: /device:TPU:16 before, /device:TPU:6 now
where the time goes in v1:
time: 121 us
  Pallas kernels  113 us (93%)
  local copies, waits for them, and re-layouts  5.73 us (5%)
  matrix products  2.53 us (2%)
    pallas_call x1, Pallas kernels, shards(): pl.pallas_call(functools.partial(kernel, n), out_shape=(jax.ShapeDtypeStr...  113 us
    unnamed x10, local copies, waits for them, and re-layouts  4.96 us
    dot_general x1, matrix products, shards(): jnp.dot(attended, weight.reshape(-1, weight.shape[2]), preferred_element_...  2.53 us

profile of v1, /device:TPU:6, one launch (start us, length us, event | category | flops | bytes accessed | tf_op | source)
XLA Modules:
  0.0 121.0 jit_solution(9409105887403111499)
XLA Ops:
  0.0 0.8 copy.7.picks_ref
  0.8 0.0 copy-start
  0.8 1.1 copy-done
  1.9 0.0 copy-start.1
  1.9 1.1 copy-done.1
  3.0 0.0 copy-start.2
  3.0 1.1 copy-done.2
  4.2 0.0 copy-start.3
  4.2 0.9 copy-done.3
  5.1 0.0 copy-start.4
  5.1 0.7 copy-done.4
  5.7 112.8 %shard_map.64 = (bf16[512,768]{1,0:T(8,128)(2,1)S(1)}, bf16[16,48,1536]{2,1,0:T(8,128)(2,1)S(1)}) custom-call(bf16[512,768]{1,0:T(8,128)(2,1)S(1)} %copy-done, bf16[4,128,768]{2,1,0:T(8,128)(2,1)S(1)} %bitcast.6, bf16[4,128,768]{2,1,0:T(8,128)(2,1)S(1)} %bitcast.7, bf16[48,1536]{1,0:T(8,128)(2,1)S(1)} %copy-done.3, s32[6,2]{1,0:T(8,128)S(1)} %copy.7.picks_ref, ...), custom_call_target="tpu_custom_call" | custom-call | tf_op jit(solution)/shard_map/pallas_call | solution.py:229
  118.5 2.5 %convolution_convert_fusion = bf16[512,1536]{1,0:T(8,128)(2,1)} fusion(bf16[512,768]{1,0:T(8,128)(2,1)S(1)} %get-tuple-element.7, bf16[768,1536]{1,0:T(8,128)(2,1)S(1)} %bitcast.8), kind=kOutput, calls=%fused_computation | convolution fusion | flops 1208745984 | bytes 4718592 | tf_op jit(solution)/shard_map/dot_general | solution.py:259
Async XLA Ops:
  0.8 1.1 copy-start
  1.9 1.1 copy-start.1
  3.0 1.1 copy-start.2
  4.2 0.9 copy-start.3
  5.1 0.7 copy-start.4

commit v2 on v1

v2 whole, which is shorter than its diff:
```python
import functools

import jax
import jax.numpy as jnp
from jax import lax
from jax.experimental import pallas as pl
from jax.experimental.pallas import tpu as pltpu
from jax.sharding import PartitionSpec as P

HD = 128
BLOCK = 128
LEVELS = 3
DIRS = 2 * LEVELS
MASKED = -1e30
LEVEL_ORDER = (1, 2, 0)


def hop(direction):
    size = 2 ** (direction % LEVELS)
    return size if direction < LEVELS else -size


def kernel(
    n, q_ref, k_ref, v_ref, w_ref, picks_ref, counts_ref, out_ref, wout_ref,
    pack, mark, got, got_mark, acc, top, total,
    pack_send, pack_recv, mark_send, mark_recv, w_send, w_recv, own_sem,
):
    me = lax.axis_index("seq")
    dp = lax.axis_index("dp")
    sibling = dp + 1 - 2 * (dp % 2)
    rows, width = q_ref.shape
    heads = width // HD
    slots = picks_ref.shape[1]
    half_cols = w_ref.shape[1] // 2
    half = pl.ds(pl.multiple_of((dp % 2) * half_cols, half_cols), half_cols)

    near = me + 1 - 2 * (me % 2)
    others = n // 2

    def inside(shard):
        return jnp.logical_and(shard >= 0, shard < n)

    barrier = pltpu.get_barrier_semaphore()
    expected = jnp.int32(others + 1)
    for direction in range(DIRS):
        other = me + hop(direction)
        expected = expected + inside(other).astype(jnp.int32)

        @pl.when(inside(other))
        def _(other=other):
            pl.semaphore_signal(
                barrier, inc=1, device_id=(dp, other), device_id_type=pl.DeviceIdType.MESH
            )
    for other in [near] + [(me + 2 * j) % n for j in range(1, others)]:
        pl.semaphore_signal(
            barrier, inc=1, device_id=(dp, other), device_id_type=pl.DeviceIdType.MESH
        )
    pl.semaphore_signal(
        barrier, inc=1, device_id=(sibling, me), device_id_type=pl.DeviceIdType.MESH
    )

    own = pltpu.make_async_copy(w_ref.at[:, half], wout_ref.at[me, :, half], own_sem)
    own.start()

    def fill(direction, slot):
        block = picks_ref[direction, slot]
        pack[direction, slot, 0] = k_ref[block]
        pack[direction, slot, 1] = v_ref[block]

    def fill_mark(direction):
        for slot in range(slots):
            live = counts_ref[0, direction] > slot
            mark[direction, slot] = jnp.full((8, HD), jnp.where(live, 0.0, MASKED), jnp.float32)

    def pack_copy(direction, slot):
        return pltpu.make_async_remote_copy(
            pack.at[direction, slot],
            got.at[direction % LEVELS, slot, :, direction // LEVELS],
            pack_send.at[direction, slot], pack_recv.at[direction, slot],
            device_id=(dp, me + hop(direction)), device_id_type=pl.DeviceIdType.MESH,
        )

    def mark_copy(direction):
        return pltpu.make_async_remote_copy(
            mark.at[direction], got_mark.at[direction],
            mark_send.at[direction], mark_recv.at[direction],
            device_id=(dp, me + hop(direction)), device_id_type=pl.DeviceIdType.MESH,
        )

    def sibling_arrival(j, same):
        shard = ((me if same else near) + n - 2 * j) % n
        other_half = pl.ds(pl.multiple_of((1 - dp % 2) * half_cols, half_cols), half_cols)
        place = wout_ref.at[shard, :, other_half]
        index = n + j + (0 if same else others)
        return pltpu.make_async_remote_copy(
            place, place, w_send.at[index], w_recv.at[index],
            device_id=(sibling, me), device_id_type=pl.DeviceIdType.MESH,
        )

    def send(level, slot):
        for direction in (level, level + LEVELS):
            fill(direction, slot)
            if slot == 0:
                fill_mark(direction)

            @pl.when(inside(me + hop(direction)))
            def _(direction=direction):
                if slot == 0:
                    mark_copy(direction).start()
                pack_copy(direction, slot).start()

    def weight_copy(shard, index, to):
        place = wout_ref.at[shard, :, half]
        return pltpu.make_async_remote_copy(
            place, place, w_send.at[index], w_recv.at[index],
            device_id=to, device_id_type=pl.DeviceIdType.MESH,
        )

    def spread(j):
        return weight_copy(me, j, (dp, (me + 2 * j) % n))

    def spread_arrival(j):
        return weight_copy((me + n - 2 * j) % n, j, (dp, (me + 2 * j) % n))

    def across(j):
        return weight_copy((me + n - 2 * j) % n, others + j, (dp, near))

    def across_arrival(j):
        return weight_copy((near + n - 2 * j) % n, others + j, (dp, near))

    def pair(j, same):
        shard = ((me if same else near) + n - 2 * j) % n
        return weight_copy(shard, n + j + (0 if same else others), (sibling, me))

    for direction in range(DIRS):

        @pl.when(jnp.logical_not(inside(me - hop(direction))))
        def _(direction=direction):
            for slot in range(slots):
                for kind in range(2):
                    got[direction % LEVELS, slot, kind, direction // LEVELS] = jnp.zeros(
                        (BLOCK, width), jnp.bfloat16
                    )
            got_mark[direction] = jnp.full((slots, 8, HD), MASKED, jnp.float32)

    pl.semaphore_wait(barrier, expected)
    own.wait()
    for j in range(1, others):
        spread(j).start()
    across(0).start()
    pair(0, True).start()
    for level in LEVEL_ORDER[:2]:
        send(level, 0)

    scale = HD**-0.5
    tiles = 2
    tile = rows // tiles

    def local_head(h, carry):
        cols = pl.ds(pl.multiple_of(h * HD, HD), HD)
        keys = k_ref[:, :, cols].reshape(rows, HD)
        values = v_ref[:, :, cols].reshape(rows, HD)
        for t in range(tiles):
            at = pl.ds(t * tile, tile)
            scores = lax.dot_general(
                q_ref[at, cols], keys, (((1,), (1,)), ((), ())),
                preferred_element_type=jnp.float32,
            ) * scale
            high = jnp.max(scores, axis=1, keepdims=True)
            weights = jnp.exp(scores - high)
            top[h, at, :] = high
            total[h, at, :] = jnp.sum(weights, axis=1, keepdims=True)
            acc[h, at, :] = jnp.dot(
                weights.astype(jnp.bfloat16), values, preferred_element_type=jnp.float32
            )
        return carry

    lax.fori_loop(0, heads // 2, local_head, 0)
    for j in range(1, others):
        spread_arrival(j).wait_recv()
        across(j).start()
        pair(j, True).start()
    for level in LEVEL_ORDER[2:]:
        send(level, 0)
    lax.fori_loop(heads // 2, heads, local_head, 0)
    send(LEVEL_ORDER[0], 1)

    def far_head(level, slot, h):
        cols = pl.ds(pl.multiple_of(h * HD, HD), HD)
        keys = got[level, slot, 0, :, :, cols].reshape(2 * BLOCK, HD)
        values = got[level, slot, 1, :, :, cols].reshape(2 * BLOCK, HD)
        bias = jnp.concatenate(
            [got_mark[direction, slot, 0:1, :] for direction in (level, level + LEVELS)], axis=1
        )
        for t in range(tiles):
            at = pl.ds(t * tile, tile)
            scores = lax.dot_general(
                q_ref[at, cols], keys, (((1,), (1,)), ((), ())),
                preferred_element_type=jnp.float32,
            ) * scale + bias
            before = top[h, at, :]
            high = jnp.maximum(before, jnp.max(scores, axis=1, keepdims=True))
            shrink = jnp.exp(before - high)
            weights = jnp.exp(scores - high)
            top[h, at, :] = high
            total[h, at, :] = total[h, at, :] * shrink + jnp.sum(weights, axis=1, keepdims=True)
            acc[h, at, :] = acc[h, at, :] * shrink + jnp.dot(
                weights.astype(jnp.bfloat16), values, preferred_element_type=jnp.float32
            )

    def far(level, slot):
        for direction in (level, level + LEVELS):

            @pl.when(inside(me - hop(direction)))
            def _(direction=direction):
                if slot == 0:
                    mark_copy(direction).wait_recv()
                pack_copy(direction, slot).wait_recv()

        def body(h, carry):
            far_head(level, slot, h)
            return carry

        lax.fori_loop(0, heads, body, 0)

    far(LEVEL_ORDER[0], 0)
    for j in range(others):
        across_arrival(j).wait_recv()
        pair(j, False).start()
    for level in LEVEL_ORDER[1:]:
        send(level, 1)
    for level in LEVEL_ORDER[1:]:
        far(level, 0)
    for slot in range(1, slots):
        for level in LEVEL_ORDER:
            far(level, slot)

    for h in range(heads):
        out_ref[:, h * HD : (h + 1) * HD] = (acc[h] / total[h]).astype(out_ref.dtype)

    for direction in range(DIRS):

        @pl.when(inside(me + hop(direction)))
        def _(direction=direction):
            mark_copy(direction).wait_send()
            for slot in range(slots):
                pack_copy(direction, slot).wait_send()

    for j in range(others):
        if j > 0:
            spread(j).wait_send()
        across(j).wait_send()
    for same in (True, False):
        for j in range(others):
            pair(j, same).wait_send()
            sibling_arrival(j, same).wait_recv()


def shards(queries, key_states, value_states, out_weight, block_picks, slot_counts):
    n = lax.axis_size("seq")
    rows, width = queries.shape
    slots = block_picks.shape[2]
    heads = width // HD
    blocks = rows // BLOCK
    vmem = pl.BlockSpec(memory_space=pltpu.VMEM)
    smem = pl.BlockSpec(memory_space=pltpu.SMEM)
    dma = pltpu.SemaphoreType.DMA
    attended, weight = pl.pallas_call(
        functools.partial(kernel, n),
        out_shape=(
            jax.ShapeDtypeStruct((rows, width), jnp.bfloat16),
            jax.ShapeDtypeStruct((n,) + out_weight.shape, jnp.bfloat16),
        ),
        in_specs=[vmem, vmem, vmem, vmem, smem, smem],
        out_specs=(vmem, pl.BlockSpec(memory_space=pl.ANY)),
        scratch_shapes=[
            pltpu.VMEM((DIRS, slots, 2, BLOCK, width), jnp.bfloat16),
            pltpu.VMEM((DIRS, slots, 8, HD), jnp.float32),
            pltpu.VMEM((LEVELS, slots, 2, 2, BLOCK, width), jnp.bfloat16),
            pltpu.VMEM((DIRS, slots, 8, HD), jnp.float32),
            pltpu.VMEM((heads, rows, HD), jnp.float32),
            pltpu.VMEM((heads, rows, 1), jnp.float32),
            pltpu.VMEM((heads, rows, 1), jnp.float32),
            dma((DIRS, slots)), dma((DIRS, slots)), dma((DIRS,)), dma((DIRS,)),
            dma((2 * n,)), dma((2 * n,)), dma,
        ],
        compiler_params=pltpu.CompilerParams(
            collective_id=0, has_side_effects=True, vmem_limit_bytes=48 * 2**20
        ),
    )(
        queries,
        key_states.reshape(blocks, BLOCK, width),
        value_states.reshape(blocks, BLOCK, width),
        out_weight,
        block_picks[0],
        slot_counts,
    )
    result = jnp.dot(
        attended, weight.reshape(-1, weight.shape[2]), preferred_element_type=jnp.float32
    )
    return result.astype(jnp.bfloat16)


def solution(mesh):
    placed = (
        P(("dp", "seq"), None),
        P(("dp", "seq"), None),
        P(("dp", "seq"), None),
        P("seq", None),
        P(("dp", "seq"), None, None),
        P(("dp", "seq"), None),
    )
    return jax.shard_map(
        shards, mesh=mesh, in_specs=placed, out_specs=P(("dp", "seq"), None), check_vma=False
    )
```

time: 121 us -> 93.6 us (0.77)
  the two profiles are of different devices: /device:TPU:6 before, /device:TPU:16 now
where the time goes in v2:
time: 93.6 us; the launch traced here: 93.3 us
  Pallas kernels  85 us (91%)
  local copies, waits for them, and re-layouts  5.73 us (6%)
  matrix products  2.53 us (3%)
    pallas_call x1, Pallas kernels, shards(): pl.pallas_call(functools.partial(kernel, n), out_shape=(jax.ShapeDtypeStr...  85 us
    unnamed x10, local copies, waits for them, and re-layouts  4.96 us
    dot_general x1, matrix products, shards(): jnp.dot(attended, weight.reshape(-1, weight.shape[2]), preferred_element_...  2.53 us

profile of v2, /device:TPU:16, one launch (start us, length us, event | category | flops | bytes accessed | tf_op | source)
XLA Modules:
  0.0 93.3 jit_solution(11740604048911498957)
XLA Ops:
  0.0 0.8 copy.7.picks_ref
  0.8 0.0 copy-start
  0.8 1.1 %copy-done = bf16[512,768]{1,0:T(8,128)(2,1)S(1)} copy-done((bf16[512,768]{1,0:T(8,128)(2,1)S(1)}, bf16[512,768]{1,0:T(8,128)(2,1)}, u32[]{:S(2)}) %copy-start) | copy-done | bytes 786456
  1.9 0.0 copy-start.1
  1.9 1.1 %copy-done.1 = bf16[512,768]{1,0:T(8,128)(2,1)S(1)} copy-done((bf16[512,768]{1,0:T(8,128)(2,1)S(1)}, bf16[512,768]{1,0:T(8,128)(2,1)}, u32[]{:S(2)}) %copy-start.1) | copy-done | bytes 786456
  3.0 0.0 copy-start.2
  3.0 1.1 %copy-done.2 = bf16[512,768]{1,0:T(8,128)(2,1)S(1)} copy-done((bf16[512,768]{1,0:T(8,128)(2,1)S(1)}, bf16[512,768]{1,0:T(8,128)(2,1)}, u32[]{:S(2)}) %copy-start.2) | copy-done | bytes 786456
  4.2 0.0 copy-start.3
  4.2 0.9 copy-done.3
  5.1 0.0 copy-start.4
  5.1 0.7 copy-done.4
  5.7 85.0 %shard_map.64 = (bf16[512,768]{1,0:T(8,128)(2,1)S(1)}, bf16[16,48,1536]{2,1,0:T(8,128)(2,1)S(1)}) custom-call(bf16[512,768]{1,0:T(8,128)(2,1)S(1)} %copy-done, bf16[4,128,768]{2,1,0:T(8,128)(2,1)S(1)} %bitcast.6, bf16[4,128,768]{2,1,0:T(8,128)(2,1)S(1)} %bitcast.7, bf16[48,1536]{1,0:T(8,128)(2,1)S(1)} %copy-done.3, s32[6,2]{1,0:T(8,128)S(1)} %copy.7.picks_ref, ...), custom_call_target="tpu_custom_call" | custom-call | tf_op jit(solution)/shard_map/pallas_call | solution.py:268
  90.8 2.5 %convolution_convert_fusion = bf16[512,1536]{1,0:T(8,128)(2,1)} fusion(bf16[512,768]{1,0:T(8,128)(2,1)S(1)} %get-tuple-element.7, bf16[768,1536]{1,0:T(8,128)(2,1)S(1)} %bitcast.8), kind=kOutput, calls=%fused_computation | convolution fusion | flops 1208745984 | bytes 4718592 | tf_op jit(solution)/shard_map/dot_general | solution.py:298
Async XLA Ops:
  0.8 1.1 %copy-start = (bf16[512,768]{1,0:T(8,128)(2,1)S(1)}, bf16[512,768]{1,0:T(8,128)(2,1)}, u32[]{:S(2)}) copy-start(bf16[512,768]{1,0:T(8,128)(2,1)} %q_ref.1) | copy-start | bytes 2359300
  1.9 1.1 %copy-start.1 = (bf16[512,768]{1,0:T(8,128)(2,1)S(1)}, bf16[512,768]{1,0:T(8,128)(2,1)}, u32[]{:S(2)}) copy-start(bf16[512,768]{1,0:T(8,128)(2,1)} %param.7) | copy-start | bytes 2359300
  3.0 1.1 %copy-start.2 = (bf16[512,768]{1,0:T(8,128)(2,1)S(1)}, bf16[512,768]{1,0:T(8,128)(2,1)}, u32[]{:S(2)}) copy-start(bf16[512,768]{1,0:T(8,128)(2,1)} %param.8) | copy-start | bytes 2359300
  4.2 0.9 copy-start.3
  5.1 0.7 copy-start.4

commit v3 on v2

--- a/solution.py
+++ b/solution.py
@@ -221,7 +221,7 @@
             far_head(level, slot, h)
             return carry
 
-        lax.fori_loop(0, heads, body, 0)
+        lax.fori_loop(0, heads, body, 0, unroll=3)
 
     far(LEVEL_ORDER[0], 0)
     for j in range(others):

time: 93.6 us -> 93.7 us (level)
  no operation moved by 1% of the time
where the time goes in v3:
time: 93.7 us; the launch traced here: 93.3 us
  Pallas kernels  85.1 us (91%)
  local copies, waits for them, and re-layouts  5.73 us (6%)
  matrix products  2.53 us (3%)
    pallas_call x1, Pallas kernels, shards(): pl.pallas_call(functools.partial(kernel, n), out_shape=(jax.ShapeDtypeStr...  85.1 us
    unnamed x10, local copies, waits for them, and re-layouts  4.96 us
    dot_general x1, matrix products, shards(): jnp.dot(attended, weight.reshape(-1, weight.shape[2]), preferred_element_...  2.53 us

profile of v3, /device:TPU:16, one launch (start us, length us, event | category | flops | bytes accessed | tf_op | source)
XLA Modules:
  0.0 93.3 jit_solution(12337280323580040971)
XLA Ops:
  0.0 0.8 copy.7.picks_ref
  0.8 0.0 copy-start
  0.8 1.1 %copy-done = bf16[512,768]{1,0:T(8,128)(2,1)S(1)} copy-done((bf16[512,768]{1,0:T(8,128)(2,1)S(1)}, bf16[512,768]{1,0:T(8,128)(2,1)}, u32[]{:S(2)}) %copy-start) | copy-done | bytes 786456
  1.9 0.0 copy-start.1
  1.9 1.1 %copy-done.1 = bf16[512,768]{1,0:T(8,128)(2,1)S(1)} copy-done((bf16[512,768]{1,0:T(8,128)(2,1)S(1)}, bf16[512,768]{1,0:T(8,128)(2,1)}, u32[]{:S(2)}) %copy-start.1) | copy-done | bytes 786456
  3.0 0.0 copy-start.2
  3.0 1.1 %copy-done.2 = bf16[512,768]{1,0:T(8,128)(2,1)S(1)} copy-done((bf16[512,768]{1,0:T(8,128)(2,1)S(1)}, bf16[512,768]{1,0:T(8,128)(2,1)}, u32[]{:S(2)}) %copy-start.2) | copy-done | bytes 786456
  4.2 0.0 copy-start.3
  4.2 0.9 copy-done.3
  5.1 0.0 copy-start.4
  5.1 0.7 copy-done.4
  5.7 85.1 %shard_map.64 = (bf16[512,768]{1,0:T(8,128)(2,1)S(1)}, bf16[16,48,1536]{2,1,0:T(8,128)(2,1)S(1)}) custom-call(bf16[512,768]{1,0:T(8,128)(2,1)S(1)} %copy-done, bf16[4,128,768]{2,1,0:T(8,128)(2,1)S(1)} %bitcast.6, bf16[4,128,768]{2,1,0:T(8,128)(2,1)S(1)} %bitcast.7, bf16[48,1536]{1,0:T(8,128)(2,1)S(1)} %copy-done.3, s32[6,2]{1,0:T(8,128)S(1)} %copy.7.picks_ref, ...), custom_call_target="tpu_custom_call" | custom-call | tf_op jit(solution)/shard_map/pallas_call | solution.py:268
  90.8 2.5 %convolution_convert_fusion = bf16[512,1536]{1,0:T(8,128)(2,1)} fusion(bf16[512,768]{1,0:T(8,128)(2,1)S(1)} %get-tuple-element.7, bf16[768,1536]{1,0:T(8,128)(2,1)S(1)} %bitcast.8), kind=kOutput, calls=%fused_computation | convolution fusion | flops 1208745984 | bytes 4718592 | tf_op jit(solution)/shard_map/dot_general | solution.py:298
Async XLA Ops:
  0.8 1.1 %copy-start = (bf16[512,768]{1,0:T(8,128)(2,1)S(1)}, bf16[512,768]{1,0:T(8,128)(2,1)}, u32[]{:S(2)}) copy-start(bf16[512,768]{1,0:T(8,128)(2,1)} %q_ref.1) | copy-start | bytes 2359300
  1.9 1.1 %copy-start.1 = (bf16[512,768]{1,0:T(8,128)(2,1)S(1)}, bf16[512,768]{1,0:T(8,128)(2,1)}, u32[]{:S(2)}) copy-start(bf16[512,768]{1,0:T(8,128)(2,1)} %param.7) | copy-start | bytes 2359300
  3.0 1.1 %copy-start.2 = (bf16[512,768]{1,0:T(8,128)(2,1)S(1)}, bf16[512,768]{1,0:T(8,128)(2,1)}, u32[]{:S(2)}) copy-start(bf16[512,768]{1,0:T(8,128)(2,1)} %param.8) | copy-start | bytes 2359300
  4.2 0.9 copy-start.3
  5.1 0.7 copy-start.4
